TPU v7x, 32 devices: a whole 2x2x4 slice. The times are simulated.
32 devices in a mesh: blk: 8 (over y, x, core), exp: 4 (over z).
Axes of the slice: x: 2, y: 2, z: 4, core: 2. Of those that a mesh axis runs over, the one named last changes fastest.
Arguments:
- residual_deposit_sequence: bfloat16 [4, 1024, 1536], P('exp', 'blk'), may hold values from -60 to 60
- premix_rescaler: float32 [1536], replicated, may hold values from 0.25 to 1.75
- asking_projector: bfloat16 [1536, 1536], P(None, 'exp'), may hold values from -0.15625 to 0.15625
- lookup_projector: bfloat16 [1536, 512], P(None, 'exp'), may hold values from -0.15625 to 0.15625
- content_projector: bfloat16 [1536, 512], P(None, 'exp'), may hold values from -0.15625 to 0.15625
- final_projector: bfloat16 [1536, 1536], P('exp'), may hold values from -0.15625 to 0.15625
- logit_multipliers: float32 [12], replicated, may hold values from 1.5 to 6
- premixture_rescaler: float32 [1536], replicated, may hold values from 0.25 to 1.75
- specialist_switch_tensor: bfloat16 [8, 1536, 384], P('exp'), may hold values from -0.15625 to 0.15625
- specialist_widen_tensor: bfloat16 [8, 1536, 384], P('exp'), may hold values from -0.15625 to 0.15625
- specialist_shrink_tensor: bfloat16 [8, 384, 1536], P('exp'), may hold values from -0.3125 to 0.3125
- picked_specialist_labels: int32 [4, 1024, 2], P(None, 'blk'), may hold values from 0 to 7, all different within a row; in each aligned block of 128 rows (0 to 127, 128 to 255, ..., all dimensions but the last counted through in order) at most 64 rows name the same one
- specialist_shares: float32 [4, 1024, 2], P(None, 'blk'), may hold values from 0.1 to 1
Outputs:
- attention_update: bfloat16 [4, 1024, 1536], P('exp', 'blk')
- expert_update: bfloat16 [4, 1024, 1536], P('exp', 'blk')
Inputs may be any that keep to these rules, and one draw needn't show every extreme that they name: `picked_specialist_labels`: the 2 ids of a hit differ. Within each event's 128 hits on one index of blk (an aligned block of 128 rows) no expert is named by more than 64 hits, a bound that some block reaches.
All inputs are finite; a program needn't handle non-finite values.
Results may differ from a plain program's by a relative error of at most 0.019.
Values may be sent and summed in bfloat16 or wider, within the bound.
A program may use at most 192 MiB of HBM per device.

v0:
```python
import math
import jax
import jax.numpy as jnp
from jax import lax
from jax.sharding import PartitionSpec as P

D = 1536
PER_LANE_DIM = 128
TOP = 2
CAP = 64


def norm_rows(values, norm_gain):
    widened = values.astype(jnp.float32)
    return (
        widened * lax.rsqrt(jnp.mean(widened * widened, axis=-1, keepdims=True) + 1e-05) * norm_gain
    )


def head_norm(values):
    return values * lax.rsqrt(jnp.mean(values * values, axis=-1, keepdims=True) + 1e-06)


def attend_hits(
    rescaled_entries,
    asking_projector,
    lookup_projector,
    content_projector,
    final_projector,
    logit_multipliers,
):
    events, row_count, model_width = rescaled_entries.shape
    common_key_heads = lookup_projector.shape[1] // PER_LANE_DIM
    local_lane_count = asking_projector.shape[1] // PER_LANE_DIM
    askers_per_lookup = local_lane_count // common_key_heads
    query_heads = jnp.einsum(
        "std,de->ste", rescaled_entries, asking_projector, preferred_element_type=jnp.float32
    )
    query_heads = head_norm(
        query_heads.reshape(events, row_count, common_key_heads, askers_per_lookup, PER_LANE_DIM)
    ).astype(jnp.bfloat16)
    key_heads = jnp.einsum(
        "std,de->ste", rescaled_entries, lookup_projector, preferred_element_type=jnp.float32
    )
    key_heads = head_norm(
        key_heads.reshape(events, row_count, common_key_heads, PER_LANE_DIM)
    ).astype(jnp.bfloat16)
    value_heads = jnp.einsum(
        "std,de->ste", rescaled_entries, content_projector, preferred_element_type=jnp.float32
    )
    value_heads = value_heads.reshape(events, row_count, common_key_heads, PER_LANE_DIM).astype(
        jnp.bfloat16
    )
    inverse_root_dim = (logit_multipliers / math.sqrt(PER_LANE_DIM)).reshape(
        common_key_heads, askers_per_lookup
    )
    key_piece = lax.all_gather(key_heads, "blk", axis=1, tiled=True)
    value_piece = lax.all_gather(value_heads, "blk", axis=1, tiled=True)
    scores = jnp.einsum(
        "sikgd,sjkd->skgij", query_heads, key_piece, preferred_element_type=jnp.float32
    )
    expo = jnp.exp(scores * inverse_root_dim[None, :, :, None, None])
    totals = jnp.sum(expo, axis=-1)
    mixture = jnp.einsum(
        "skgij,sjkd->skgid",
        expo.astype(jnp.bfloat16),
        value_piece,
        preferred_element_type=jnp.float32,
    )
    totals, mixture = (totals, mixture)
    heads_out = head_norm(mixture / totals[..., None]).astype(jnp.bfloat16)
    out_blocks = final_projector.reshape(
        common_key_heads, askers_per_lookup, PER_LANE_DIM, model_width
    )
    return jnp.einsum("skgid,kgde->sie", heads_out, out_blocks, preferred_element_type=jnp.float32)


def slot_tables(chosen, expert_count):
    events, row_count, top_count = chosen.shape
    flat_ids = chosen.reshape(events, row_count * top_count)
    onehot = (
        flat_ids[:, :, None] == jnp.arange(expert_count, dtype=jnp.int32)[None, None, :]
    ).astype(jnp.int32)
    before = jnp.cumsum(onehot, axis=1) - onehot
    slot_of = jnp.sum(before * onehot, axis=2)
    source_rows = jnp.arange(row_count * top_count, dtype=jnp.int32)[None, :] // top_count
    event_index = jnp.arange(events, dtype=jnp.int32)[:, None]
    tables = (
        jnp.zeros((events, expert_count, CAP), jnp.int32)
        .at[event_index, flat_ids, slot_of]
        .set(source_rows)
    )
    return (slot_of, tables)


def run_experts(
    batched, specialist_switch_tensor, specialist_widen_tensor, specialist_shrink_tensor
):
    gate_act = jnp.einsum(
        "sjcd,jdf->sjcf", batched, specialist_switch_tensor, preferred_element_type=jnp.float32
    )
    up_act = jnp.einsum(
        "sjcd,jdf->sjcf", batched, specialist_widen_tensor, preferred_element_type=jnp.float32
    )
    hidden = (jax.nn.silu(gate_act) * up_act).astype(jnp.bfloat16)
    return jnp.einsum(
        "sjcf,jfd->sjcd", hidden, specialist_shrink_tensor, preferred_element_type=jnp.float32
    ).astype(jnp.bfloat16)


def body(
    residual_deposit_sequence,
    premix_rescaler,
    asking_projector,
    lookup_projector,
    content_projector,
    final_projector,
    logit_multipliers,
    premixture_rescaler,
    specialist_switch_tensor,
    specialist_widen_tensor,
    specialist_shrink_tensor,
    picked_specialist_labels,
    specialist_shares,
):
    specialist_slot = lax.axis_index("exp")
    exp_count = lax.axis_size("exp")
    rows_all = lax.all_gather(residual_deposit_sequence, "exp", axis=0, tiled=True)
    rescaled_entries = norm_rows(rows_all, premix_rescaler).astype(jnp.bfloat16)
    local_lane_count = asking_projector.shape[1] // PER_LANE_DIM
    device_scratch = lax.dynamic_slice_in_dim(
        logit_multipliers, specialist_slot * local_lane_count, local_lane_count
    )
    partial_out = attend_hits(
        rescaled_entries,
        asking_projector,
        lookup_projector,
        content_projector,
        final_projector,
        device_scratch,
    )
    attention_full = lax.psum_scatter(
        partial_out.astype(jnp.bfloat16), "exp", scatter_dimension=0, tiled=True
    ).astype(jnp.float32)
    attention_update = attention_full.astype(jnp.bfloat16)
    residual = residual_deposit_sequence.astype(jnp.float32) + attention_full
    expert_in = norm_rows(residual, premixture_rescaler).astype(jnp.bfloat16)
    row_count = expert_in.shape[1]
    local_experts = specialist_switch_tensor.shape[0]
    expert_count = local_experts * exp_count
    own_ids = lax.dynamic_slice_in_dim(picked_specialist_labels, specialist_slot, 1, 0)
    own_gates = lax.dynamic_slice_in_dim(specialist_shares, specialist_slot, 1, 0).reshape(
        row_count * TOP
    )
    slot_of, tables = slot_tables(own_ids, expert_count)
    outgoing = jnp.take(expert_in[0], tables[0].reshape(expert_count * CAP), axis=0)
    outgoing = outgoing.reshape(exp_count, local_experts, CAP, D)
    produced = run_experts(
        lax.all_to_all(outgoing, "exp", split_axis=0, concat_axis=0, tiled=True),
        specialist_switch_tensor,
        specialist_widen_tensor,
        specialist_shrink_tensor,
    )
    returned = lax.all_to_all(produced, "exp", split_axis=0, concat_axis=0, tiled=True)
    position = own_ids.reshape(row_count * TOP) * CAP + slot_of[0]
    values = jnp.take(returned.reshape(expert_count * CAP, D), position, axis=0).astype(jnp.float32)
    combined = jnp.sum((values * own_gates[:, None]).reshape(row_count, TOP, D), axis=1)
    expert_update = combined.astype(jnp.bfloat16)[None]
    return (attention_update, expert_update)


def solution(mesh):
    placed = (
        P("exp", "blk", None),
        P(),
        P(None, "exp"),
        P(None, "exp"),
        P(None, "exp"),
        P("exp", None),
        P(),
        P(),
        P("exp", None, None),
        P("exp", None, None),
        P("exp", None, None),
        P(None, "blk", None),
        P(None, "blk", None),
    )
    return jax.shard_map(
        body,
        mesh=mesh,
        in_specs=placed,
        out_specs=(P("exp", "blk", None), P("exp", "blk", None)),
        check_vma=False,
    )
```

profile of v0, /device:TPU:0, one launch (start us, length us, event | category | flops | bytes accessed | tf_op | source)
XLA Modules:
  0.0 258.9 jit_solution(3094345826512784104)
XLA Ops:
  8.0 41.4 %all-gather.6.cloned.1.call-done = bf16[4,128,1536]{2,1,0:T(8,128)(2,1)} async-done(((bf16[1,128,1536]{2,1,0:T(8,128)(2,1)}), bf16[4,128,1536]{2,1,0:T(8,128)(2,1)}) %all-gather.6.cloned.1.call-update) | async-done | bytes 1572880 | tf_op jit(solution)/shard_map/all_gather | solution.py:128
  49.4 1.9 fusion.1
  51.4 1.5 multiply_reduce_fusion.3
  53.7 2.7 %convolution_convert_fusion.1 = bf16[4,128,128]{2,1,0:T(8,128)(2,1)} fusion(bf16[4,128,1536]{2,1,0:T(8,128)(2,1)} %all-gather.6.cloned.1.call-done, f32[1536]{0:T(1024)S(1)} %copy-done.9, f32[4,128]{1,0:T(4,128)S(1)} %add_rsqrt_fusion.3, bf16[1536,128]{1,0:T(8,128)(2,1)S(1)} %copy-done.8), kind=kOutput, calls=%fused_computation.35 | convolution fusion | flops 204537856 | bytes 2105344 | tf_op jit(solution)/shard_map/std,de->ste/dot_general | solution.py:48
  56.6 3.7 %fusion.70 = (f32[4,128,384]{2,1,0:T(8,128)S(1)}, f32[4,128,384]{2,1,0:T(8,128)}) fusion(bf16[1536,384]{1,0:T(8,128)(2,1)} %param.15, bf16[4,128,1536]{2,1,0:T(8,128)(2,1)} %all-gather.6.cloned.1.call-done, f32[1536]{0:T(1024)S(1)} %copy-done.9, f32[4,128]{1,0:T(4,128)S(1)} %add_rsqrt_fusion.3), kind=kOutput, calls=%fused_computation.101 | convolution fusion | flops 607322112 | bytes 4333568 | tf_op jit(solution)/shard_map/std,de->ste/dot_general | solution.py:36
  61.4 1.4 copy.52
  64.0 12.2 %all-gather.8.cloned.1.call-done = bf16[4,1024,128]{1,2,0:T(8,128)(2,1)} async-done(((bf16[4,128,128]{1,2,0:T(8,128)(2,1)}), bf16[4,1024,128]{1,2,0:T(8,128)(2,1)}) %all-gather.8.cloned.1.call-update) | async-done | bytes 1048592 | tf_op jit(solution)/shard_map/all_gather | solution.py:57
  76.2 5.4 %bitcast_reduce_fusion = (f32[4,3,128]{2,1,0:T(4,128)S(1)}, f32[4,1024,128,3]{2,1,3,0:T(8,128)}) fusion(f32[3]{0:T(128)S(1)} %dynamic-slice_multiply_fusion, f32[4,128,3,128]{1,3,2,0:T(8,128)S(1)} %bitcast.150, f32[4,128,3]{1,2,0:T(4,128)S(1)} %add_rsqrt_fusion.1, bf16[4,1024,128]{1,2,0:T(8,128)(2,1)} %all-gather.8.cloned.1.call-done), kind=kOutput, calls=%fused_computation.3 | convolution fusion | flops 406190592 | bytes 8138764 | tf_op jit(solution)/shard_map/sikgd,sjkd->skgij/dot_general | solution.py:59
  81.6 20.6 %all-gather.10.cloned.1.call-done = bf16[4,1024,128]{2,1,0:T(8,128)(2,1)} async-done(((bf16[4,128,128]{2,1,0:T(8,128)(2,1)}), bf16[4,1024,128]{2,1,0:T(8,128)(2,1)}) %all-gather.10.cloned.1.call-update) | async-done | bytes 1048592 | tf_op jit(solution)/shard_map/all_gather | solution.py:58
  102.2 4.4 %multiply_reduce_fusion.2 = (f32[4,3,128]{2,1,0:T(4,128)S(1)}, f32[4,3,128,128]{2,3,1,0:T(8,128)S(1)}) fusion(f32[4,3,128]{2,1,0:T(4,128)S(1)} %get-tuple-element.8, bf16[4,1024,128]{2,1,0:T(8,128)(2,1)} %all-gather.10.cloned.1.call-done, f32[4,1024,128,3]{2,1,3,0:T(8,128)} %get-tuple-element.9, f32[3]{0:T(128)S(1)} %dynamic-slice_multiply_fusion), kind=kOutput, calls=%fused_computation.50 | convolution fusion | flops 406387200 | bytes 8138764 | tf_op jit(solution)/shard_map/skgij,sjkd->skgid/dot_general | solution.py:64
  106.7 2.2 fusion.8
  111.1 11.2 %scatter_fusion = s32[8,64]{1,0:T(8,128)S(1)} fusion(s32[8,64]{1,0:T(8,128)S(1)} %broadcast.318, s32[256]{0:T(256)S(1)} %bitcast.148, s32[256]{0:T(256)S(1)} %bitcast.159), kind=kCustom, calls=%fused_computation.2 | custom fusion | bytes 5120 | tf_op jit(solution)/shard_map/scatter | solution.py:91
  122.4 22.0 %reduce-scatter.2.cloned.1.call-done = bf16[1,128,1536]{2,1,0:T(8,128)(2,1)} async-done(((bf16[4,128,1536]{2,1,0:T(8,128)(2,1)}), bf16[1,128,1536]{2,1,0:T(8,128)(2,1)}) %reduce-scatter.2.cloned.1.call-update) | async-done | bytes 393232 | tf_op jit(solution)/shard_map/reduce_scatter | solution.py:142
  144.3 1.2 multiply_reduce_fusion.1
  146.7 3.0 %gather_fusion = bf16[512,1536]{1,0:T(8,128)(2,1)} fusion(bf16[128,1536]{1,0:T(8,128)(2,1)S(1)} %fusion.60, s32[1024]{0:T(1024)S(1)} %pad_clamp_fusion.1), kind=kCustom, calls=%fused_computation | custom fusion | bytes 3147776 | tf_op jit(solution)/shard_map/jit(_take)/gather | solution.py:156
  149.7 1.6 broadcast_select_fusion
  151.3 39.7 %all_to_all.10 = bf16[4,2,64,1536]{3,2,1,0:T(8,128)(2,1)S(1)} all-to-all(bf16[4,2,64,1536]{3,2,1,0:T(8,128)(2,1)S(1)} %broadcast_select_fusion), channel_id=1, replica_groups=mesh['blk'=8,'exp'=4] {'exp'}, dimensions={0} | all-to-all | bytes 3145728 | tf_op jit(solution)/shard_map/all_to_all | solution.py:159
  193.2 5.1 %fusion.9 = bf16[4,2,64,1536]{3,2,0,1:T(8,128)(2,1)} fusion(bf16[2,384,1536]{2,1,0:T(8,128)(2,1)S(1)} %copy-done, bf16[2,1536,384]{2,1,0:T(8,128)(2,1)} %param.22, bf16[4,2,64,1536]{3,2,1,0:T(8,128)(2,1)} %copy-done.3, f32[4,2,64,384]{3,2,0,1:T(8,128)S(1)} %fusion.17), kind=kOutput, calls=%fused_computation.18 | convolution fusion | flops 1209925632 | bytes 8650752 | tf_op jit(solution)/shard_map/sjcf,jfd->sjcd/dot_general | solution.py:106
  198.3 2.7 %copy.65 = bf16[4,2,64,1536]{3,2,1,0:T(8,128)(2,1)} copy(bf16[4,2,64,1536]{3,2,0,1:T(8,128)(2,1)} %fusion.9) | data formatting | bytes 3145728 | tf_op jit(solution)/shard_map/convert_element_type | solution.py:108
  200.9 4.3 %all-to-all-start.1 = ((bf16[4,2,64,1536]{3,2,1,0:T(8,128)(2,1)}), bf16[4,2,64,1536]{3,2,1,0:T(8,128)(2,1)}, u32[]{:S(2)}, u32[]{:S(2)}) async-start(bf16[4,2,64,1536]{3,2,1,0:T(8,128)(2,1)} %copy.65), calls=%async_computation.2 | async-start | bytes 3145728 | tf_op jit(solution)/shard_map/all_to_all | solution.py:164
  206.7 35.1 %all-to-all-done.1 = bf16[4,2,64,1536]{3,2,1,0:T(8,128)(2,1)} async-done(((bf16[4,2,64,1536]{3,2,1,0:T(8,128)(2,1)}), bf16[4,2,64,1536]{3,2,1,0:T(8,128)(2,1)}, u32[]{:S(2)}, u32[]{:S(2)}) %all-to-all-start.1) | async-done | bytes 1572896 | tf_op jit(solution)/shard_map/all_to_all | solution.py:164
  241.8 4.5 %gather_fusion.1 = bf16[256,1536]{1,0:T(8,128)(2,1)} fusion(bf16[512,1536]{1,0:T(8,128)(2,1)} %bitcast.38, s32[1024]{0:T(1024)S(1)} %pad_clamp_fusion), kind=kCustom, calls=%fused_computation.1 | custom fusion | bytes 1573888 | tf_op jit(solution)/shard_map/jit(_take)/gather | solution.py:166
  246.3 2.2 gather.15
  248.4 3.9 %multiply_reduce_fusion = bf16[128,1536]{1,0:T(8,128)(2,1)} fusion(bf16[128,2,1536]{2,1,0:T(2,128)(2,1)S(1)} %gather.15, pred[128,2]{1,0:T(8,128)(4,1)S(1)} %copy.61, f32[128,2]{1,0:T(8,128)S(1)} %copy.67), kind=kLoop, calls=%fused_computation.24 | loop fusion | flops 1376256 | bytes 1180928 | tf_op jit(solution)/shard_map/reduce_sum | solution.py:167
  (71 shorter events, 11.0 us)
Async XLA Ops:
  7.2 186.0 %copy-start = (bf16[2,384,1536]{2,1,0:T(8,128)(2,1)S(1)}, bf16[2,384,1536]{2,1,0:T(8,128)(2,1)}, u32[]{:S(2)}) copy-start(bf16[2,384,1536]{2,1,0:T(8,128)(2,1)} %param.23) | copy-start | bytes 7077892
  7.2 44.2 %copy-start.7 = (bf16[1536,128]{1,0:T(8,128)(2,1)S(1)}, bf16[1536,128]{1,0:T(8,128)(2,1)}, u32[]{:S(2)}) copy-start(bf16[1536,128]{1,0:T(8,128)(2,1)} %param.16) | copy-start | bytes 1179652
  7.2 42.2 %all-gather.6.cloned.1.call-start = ((), (), s32[]{:S(2)}) async-start(), calls=%async_computation.3 | async-start | bytes 1966080 | tf_op jit(solution)/shard_map/all_gather | solution.py:128
  7.9 68.3 %all-gather.8.cloned.1.call-start = ((), (), s32[]{:S(2)}) async-start(), calls=%async_computation.5 | async-start | bytes 1179648 | tf_op jit(solution)/shard_map/all_gather | solution.py:57
  49.4 1.9 copy-start.2
  51.4 2.3 copy-start.8
  51.4 2.3 copy-start.9
  53.6 2.9 %copy-start.10 = (f32[12]{0:T(128)S(1)}, f32[12]{0:T(128)}, u32[]{:S(2)}) copy-start(f32[12]{0:T(128)} %param.19) | copy-start | bytes 148
  53.6 48.6 %all-gather.10.cloned.1.call-start = ((), (), s32[]{:S(2)}) async-start(), calls=%async_computation.6 | async-start | bytes 1179648 | tf_op jit(solution)/shard_map/all_gather | solution.py:58
  56.4 87.9 %reduce-scatter.2.cloned.1.call-start = ((), (), s32[]{:S(2)}) async-start(), calls=%async_computation.4 | async-start | bytes 1966080 | tf_op jit(solution)/shard_map/reduce_scatter | solution.py:142
  102.2 4.5 %copy-start.4 = (bf16[384,1536]{1,0:T(8,128)(2,1)S(1)}, bf16[384,1536]{1,0:T(8,128)(2,1)}, u32[]{:S(2)}) copy-start(bf16[384,1536]{1,0:T(8,128)(2,1)} %param.18) | copy-start | bytes 3538948
  108.9 35.4 %copy-start.1 = (bf16[1,128,1536]{2,1,0:T(8,128)(2,1)S(1)}, bf16[1,128,1536]{2,1,0:T(8,128)(2,1)}, u32[]{:S(2)}) copy-start(bf16[1,128,1536]{2,1,0:T(8,128)(2,1)} %param.13) | copy-start | bytes 1179652
  110.0 35.5 %copy-start.5 = (f32[1536]{0:T(1024)S(1)}, f32[1536]{0:T(1024)}, u32[]{:S(2)}) copy-start(f32[1536]{0:T(1024)} %param.20) | copy-start | bytes 18436
  151.3 40.8 %copy-start.6 = (bf16[2,1536,384]{2,1,0:T(8,128)(2,1)S(1)}, bf16[2,1536,384]{2,1,0:T(8,128)(2,1)}, u32[]{:S(2)}) copy-start(bf16[2,1536,384]{2,1,0:T(8,128)(2,1)} %param.21) | copy-start | bytes 7077892
  191.0 1.1 copy-start.3
  200.9 40.9 %all-to-all-start.1 = ((bf16[4,2,64,1536]{3,2,1,0:T(8,128)(2,1)}), bf16[4,2,64,1536]{3,2,1,0:T(8,128)(2,1)}, u32[]{:S(2)}, u32[]{:S(2)}) async-start(bf16[4,2,64,1536]{3,2,1,0:T(8,128)(2,1)} %copy.65), calls=%async_computation.2 | async-start | bytes 3145728 | tf_op jit(solution)/shard_map/all_to_all | solution.py:164
Sparse Core Ops, SparseCore 0:
  9.6 39.7 all-gather.5
  53.8 22.4 all-gather.7
  78.7 23.4 all-gather.9
  109.0 35.2 reduce-scatter.1
where the time goes:
time: 260 us; the launch traced here: 259 us
  waiting for transfers between devices  132 us (51%)
  blocking collectives  39.7 us (15%)
  local copies, waits for them, and re-layouts  29.3 us (11%)
  matrix products  26 us (10%)
  between operations  14.1 us (5%)
  other arithmetic  13.3 us (5%)
  starting transfers between devices  4.49 us (2%)
    all_gather x1, waiting for transfers between devices, body(): lax.all_gather(residual_deposit_sequence, 'exp', axis=0, tiled=True)  41.4 us
    all_to_all x1, blocking collectives, body(): lax.all_to_all(outgoing, 'exp', split_axis=0, concat_axis=0, tiled=True)  39.7 us
    all_to_all x1, waiting for transfers between devices, body(): lax.all_to_all(produced, 'exp', split_axis=0, concat_axis=0, tiled=True)  35.1 us
    reduce_scatter x1, waiting for transfers between devices, body(): lax.psum_scatter(partial_out.astype(jnp.bfloat16), 'exp', scatter_dimensi...  22 us
    all_gather x1, waiting for transfers between devices, attend_hits(): value_piece = lax.all_gather(value_heads, 'blk', axis=1, tiled=True)  20.6 us
    all_gather x1, waiting for transfers between devices, attend_hits(): key_piece = lax.all_gather(key_heads, 'blk', axis=1, tiled=True)  12.2 us
    scatter x1, local copies, waits for them, and re-layouts, slot_tables(): tables = jnp.zeros((events, expert_count, CAP), jnp.int32).at[event_index...  11.2 us
    gather x2, local copies, waits for them, and re-layouts, body(): jnp.take(returned.reshape(expert_count * CAP, D), position, axis=0)  6.65 us
  transfers between devices with their start and end apart: 5, of which 5 were waited for; matrix products, arithmetic and copies ran while one was open for 12% of the time, Pallas kernels for 0%

commit v1 on v0

--- a/solution.py
+++ b/solution.py
@@ -54,8 +54,9 @@
     inverse_root_dim = (logit_multipliers / math.sqrt(PER_LANE_DIM)).reshape(
         common_key_heads, askers_per_lookup
     )
-    key_piece = lax.all_gather(key_heads, "blk", axis=1, tiled=True)
-    value_piece = lax.all_gather(value_heads, "blk", axis=1, tiled=True)
+    taken_in = jnp.concatenate([key_heads, value_heads], axis=0)
+    part_now = lax.all_gather(taken_in, "blk", axis=1, tiled=True)
+    key_piece, value_piece = jnp.split(part_now, [key_heads.shape[0]], axis=0)
     scores = jnp.einsum(
         "sikgd,sjkd->skgij", query_heads, key_piece, preferred_element_type=jnp.float32
     )

time: 260 us -> 239 us (0.919)
  waiting for transfers between devices: 132 us -> 119 us
  matrix products: 26 us -> 18.6 us
    all_gather x2 -> x1, waiting for transfers between devices: 32.8 us -> 19.6 us  [attend_hits(): part_now = lax.all_gather(taken_in, 'blk', axis=1, tiled=True)]
    dot_general x1, matrix products: 4.44 us -> 1.44 us  [attend_hits(): jnp.einsum('skgij,sjkd->skgid', expo.astype(jnp.bfloat16), value_piece, p...]
  transfers between devices with their start and end apart: 5 -> 4, of which waited for: 5 -> 4; matrix products, arithmetic and copies ran while one was open for 12% -> 9% of each run, Pallas kernels for 0% -> 0%
where the time goes in v1:
time: 239 us; the launch traced here: 238 us
  waiting for transfers between devices  119 us (50%)
  blocking collectives  39.7 us (17%)
  local copies, waits for them, and re-layouts  29.3 us (12%)
  matrix products  18.6 us (8%)
  between operations  14.1 us (6%)
  other arithmetic  13.4 us (6%)
  starting transfers between devices  4.45 us (2%)
    all_gather x1, waiting for transfers between devices, body(): lax.all_gather(residual_deposit_sequence, 'exp', axis=0, tiled=True)  41.4 us
    all_to_all x1, blocking collectives, body(): lax.all_to_all(outgoing, 'exp', split_axis=0, concat_axis=0, tiled=True)  39.7 us
    all_to_all x1, waiting for transfers between devices, body(): lax.all_to_all(produced, 'exp', split_axis=0, concat_axis=0, tiled=True)  35.1 us
    reduce_scatter x1, waiting for transfers between devices, body(): lax.psum_scatter(partial_out.astype(jnp.bfloat16), 'exp', scatter_dimensi...  22 us
    all_gather x1, waiting for transfers between devices, attend_hits(): part_now = lax.all_gather(taken_in, 'blk', axis=1, tiled=True)  19.6 us
    scatter x1, local copies, waits for them, and re-layouts, slot_tables(): tables = jnp.zeros((events, expert_count, CAP), jnp.int32).at[event_index...  11.2 us
    gather x2, local copies, waits for them, and re-layouts, body(): jnp.take(returned.reshape(expert_count * CAP, D), position, axis=0)  6.65 us
    dot_general x1, matrix products, run_experts(): jnp.einsum('sjcf,jfd->sjcd', hidden, specialist_shrink_tensor, preferred_...  5.1 us
  transfers between devices with their start and end apart: 4, of which 4 were waited for; matrix products, arithmetic and copies ran while one was open for 9% of the time, Pallas kernels for 0%

profile of v1, /device:TPU:0, one launch (start us, length us, event | category | flops | bytes accessed | tf_op | source)
XLA Modules:
  0.0 238.3 jit_solution(12476343048516355148)
XLA Ops:
  8.0 41.4 %all-gather.3.cloned.1.call-done = bf16[4,128,1536]{2,1,0:T(8,128)(2,1)} async-done(((bf16[1,128,1536]{2,1,0:T(8,128)(2,1)}), bf16[4,128,1536]{2,1,0:T(8,128)(2,1)}) %all-gather.3.cloned.1.call-update) | async-done | bytes 1572880 | tf_op jit(solution)/shard_map/all_gather | solution.py:129
  49.4 1.9 fusion.1
  51.4 1.5 multiply_reduce_fusion.3
  54.7 3.7 %fusion.68 = (f32[4,128,384]{2,1,0:T(8,128)S(1)}, f32[4,128,384]{2,1,0:T(8,128)}) fusion(bf16[1536,384]{1,0:T(8,128)(2,1)} %param.15, bf16[4,128,1536]{2,1,0:T(8,128)(2,1)} %all-gather.3.cloned.1.call-done, f32[1536]{0:T(1024)S(1)} %copy-done.10, f32[4,128]{1,0:T(4,128)S(1)} %add_rsqrt_fusion.3), kind=kOutput, calls=%fused_computation.104 | convolution fusion | flops 607322112 | bytes 4333568 | tf_op jit(solution)/shard_map/std,de->ste/dot_general | solution.py:36
  58.3 1.2 copy.56
  59.5 1.4 copy.55
  60.9 1.2 reduce_sum.80
  62.2 19.6 %all-gather.5.cloned.1.call-done = bf16[8,1024,1,128]{1,3,0,2:T(8,128)(2,1)} async-done(((bf16[8,128,1,128]{1,3,0,2:T(8,128)(2,1)}), bf16[8,1024,1,128]{1,3,0,2:T(8,128)(2,1)}) %all-gather.5.cloned.1.call-update) | async-done | bytes 2097168 | tf_op jit(solution)/shard_map/all_gather | solution.py:58
  81.7 3.0 %bitcast_reduce_fusion = (f32[4,3,128]{2,1,0:T(4,128)S(1)}, f32[4,1024,128,3]{2,1,3,0:T(8,128)S(1)}) fusion(f32[3]{0:T(128)S(1)} %dynamic-slice_multiply_fusion, f32[4,128,3,128]{1,3,2,0:T(8,128)S(1)} %bitcast.156, f32[4,128,3]{1,2,0:T(4,128)S(1)} %add_rsqrt_fusion.1, bf16[8,1024,1,128]{1,3,0,2:T(8,128)(2,1)} %all-gather.5.cloned.1.call-done), kind=kOutput, calls=%fused_computation.3 | convolution fusion | flops 406190592 | bytes 8138764 | tf_op jit(solution)/shard_map/sikgd,sjkd->skgij/dot_general | solution.py:60
  84.7 1.4 multiply_reduce_fusion.2
  86.2 2.2 fusion.8
  90.6 11.2 %scatter_fusion = s32[8,64]{1,0:T(8,128)S(1)} fusion(s32[8,64]{1,0:T(8,128)S(1)} %broadcast.318, s32[256]{0:T(256)S(1)} %bitcast.154, s32[256]{0:T(256)S(1)} %bitcast.165), kind=kCustom, calls=%fused_computation.2 | custom fusion | bytes 5120 | tf_op jit(solution)/shard_map/scatter | solution.py:92
  101.9 22.0 %reduce-scatter.2.cloned.1.call-done = bf16[1,128,1536]{2,1,0:T(8,128)(2,1)} async-done(((bf16[4,128,1536]{2,1,0:T(8,128)(2,1)}), bf16[1,128,1536]{2,1,0:T(8,128)(2,1)}) %reduce-scatter.2.cloned.1.call-update) | async-done | bytes 393232 | tf_op jit(solution)/shard_map/reduce_scatter | solution.py:143
  123.8 1.2 multiply_reduce_fusion.1
  126.2 3.0 %gather_fusion = bf16[512,1536]{1,0:T(8,128)(2,1)} fusion(bf16[128,1536]{1,0:T(8,128)(2,1)S(1)} %fusion.57, s32[1024]{0:T(1024)S(1)} %pad_clamp_fusion.1), kind=kCustom, calls=%fused_computation | custom fusion | bytes 3147776 | tf_op jit(solution)/shard_map/jit(_take)/gather | solution.py:157
  129.2 1.6 broadcast_select_fusion
  130.8 39.7 %all_to_all.10 = bf16[4,2,64,1536]{3,2,1,0:T(8,128)(2,1)S(1)} all-to-all(bf16[4,2,64,1536]{3,2,1,0:T(8,128)(2,1)S(1)} %broadcast_select_fusion), channel_id=1, replica_groups=mesh['blk'=8,'exp'=4] {'exp'}, dimensions={0} | all-to-all | bytes 3145728 | tf_op jit(solution)/shard_map/all_to_all | solution.py:160
  172.6 5.1 %fusion.9 = bf16[4,2,64,1536]{3,2,0,1:T(8,128)(2,1)} fusion(bf16[2,384,1536]{2,1,0:T(8,128)(2,1)S(1)} %copy-done, bf16[2,1536,384]{2,1,0:T(8,128)(2,1)} %param.22, bf16[4,2,64,1536]{3,2,1,0:T(8,128)(2,1)} %copy-done.3, f32[4,2,64,384]{3,2,0,1:T(8,128)S(1)} %fusion.17), kind=kOutput, calls=%fused_computation.18 | convolution fusion | flops 1209925632 | bytes 8650752 | tf_op jit(solution)/shard_map/sjcf,jfd->sjcd/dot_general | solution.py:107
  177.7 2.7 %copy.67 = bf16[4,2,64,1536]{3,2,1,0:T(8,128)(2,1)} copy(bf16[4,2,64,1536]{3,2,0,1:T(8,128)(2,1)} %fusion.9) | data formatting | bytes 3145728 | tf_op jit(solution)/shard_map/convert_element_type | solution.py:109
  180.4 4.3 %all-to-all-start.1 = ((bf16[4,2,64,1536]{3,2,1,0:T(8,128)(2,1)}), bf16[4,2,64,1536]{3,2,1,0:T(8,128)(2,1)}, u32[]{:S(2)}, u32[]{:S(2)}) async-start(bf16[4,2,64,1536]{3,2,1,0:T(8,128)(2,1)} %copy.67), calls=%async_computation.2 | async-start | bytes 3145728 | tf_op jit(solution)/shard_map/all_to_all | solution.py:165
  186.2 35.1 %all-to-all-done.1 = bf16[4,2,64,1536]{3,2,1,0:T(8,128)(2,1)} async-done(((bf16[4,2,64,1536]{3,2,1,0:T(8,128)(2,1)}), bf16[4,2,64,1536]{3,2,1,0:T(8,128)(2,1)}, u32[]{:S(2)}, u32[]{:S(2)}) %all-to-all-start.1) | async-done | bytes 1572896 | tf_op jit(solution)/shard_map/all_to_all | solution.py:165
  221.3 4.5 %gather_fusion.1 = bf16[256,1536]{1,0:T(8,128)(2,1)} fusion(bf16[512,1536]{1,0:T(8,128)(2,1)} %bitcast.43, s32[1024]{0:T(1024)S(1)} %pad_clamp_fusion), kind=kCustom, calls=%fused_computation.1 | custom fusion | bytes 1573888 | tf_op jit(solution)/shard_map/jit(_take)/gather | solution.py:167
  225.8 2.2 gather.15
  227.9 3.9 %multiply_reduce_fusion = bf16[128,1536]{1,0:T(8,128)(2,1)} fusion(bf16[128,2,1536]{2,1,0:T(2,128)(2,1)S(1)} %gather.15, pred[128,2]{1,0:T(8,128)(4,1)S(1)} %copy.63, f32[128,2]{1,0:T(8,128)S(1)} %copy.69), kind=kLoop, calls=%fused_computation.24 | loop fusion | flops 1376256 | bytes 1180928 | tf_op jit(solution)/shard_map/reduce_sum | solution.py:168
  (71 shorter events, 9.5 us)
Async XLA Ops:
  7.2 165.5 %copy-start = (bf16[2,384,1536]{2,1,0:T(8,128)(2,1)S(1)}, bf16[2,384,1536]{2,1,0:T(8,128)(2,1)}, u32[]{:S(2)}) copy-start(bf16[2,384,1536]{2,1,0:T(8,128)(2,1)} %param.23) | copy-start | bytes 7077892
  7.2 44.2 %copy-start.8 = (bf16[1536,128]{1,0:T(8,128)(2,1)S(1)}, bf16[1536,128]{1,0:T(8,128)(2,1)}, u32[]{:S(2)}) copy-start(bf16[1536,128]{1,0:T(8,128)(2,1)} %param.16) | copy-start | bytes 1179652
  7.2 42.2 %all-gather.3.cloned.1.call-start = ((), (), s32[]{:S(2)}) async-start(), calls=%async_computation.3 | async-start | bytes 1966080 | tf_op jit(solution)/shard_map/all_gather | solution.py:129
  7.9 73.8 %all-gather.5.cloned.1.call-start = ((), (), s32[]{:S(2)}) async-start(), calls=%async_computation.4 | async-start | bytes 2359296 | tf_op jit(solution)/shard_map/all_gather | solution.py:58
  49.4 1.9 copy-start.2
  51.4 1.6 copy-start.9
  51.4 1.6 copy-start.10
  53.0 1.6 copy-start.11
  54.5 69.3 %reduce-scatter.2.cloned.1.call-start = ((), (), s32[]{:S(2)}) async-start(), calls=%async_computation.5 | async-start | bytes 1966080 | tf_op jit(solution)/shard_map/reduce_scatter | solution.py:143
  81.7 3.0 %copy-start.5 = (bf16[8,1024,1,128]{1,3,0,2:T(8,128)(2,1)S(1)}, bf16[8,1024,1,128]{1,3,0,2:T(8,128)(2,1)}, u32[]{:S(2)}) copy-start(bf16[8,1024,1,128]{1,3,0,2:T(8,128)(2,1)} %all-gather.5.cloned.1.call-done) | copy-start | bytes 6291460
  84.7 1.5 copy-start.4
  88.4 35.4 %copy-start.1 = (bf16[1,128,1536]{2,1,0:T(8,128)(2,1)S(1)}, bf16[1,128,1536]{2,1,0:T(8,128)(2,1)}, u32[]{:S(2)}) copy-start(bf16[1,128,1536]{2,1,0:T(8,128)(2,1)} %param.13) | copy-start | bytes 1179652
  89.5 35.5 %copy-start.6 = (f32[1536]{0:T(1024)S(1)}, f32[1536]{0:T(1024)}, u32[]{:S(2)}) copy-start(f32[1536]{0:T(1024)} %param.20) | copy-start | bytes 18436
  130.8 40.8 %copy-start.7 = (bf16[2,1536,384]{2,1,0:T(8,128)(2,1)S(1)}, bf16[2,1536,384]{2,1,0:T(8,128)(2,1)}, u32[]{:S(2)}) copy-start(bf16[2,1536,384]{2,1,0:T(8,128)(2,1)} %param.21) | copy-start | bytes 7077892
  170.5 1.1 copy-start.3
  180.4 40.9 %all-to-all-start.1 = ((bf16[4,2,64,1536]{3,2,1,0:T(8,128)(2,1)}), bf16[4,2,64,1536]{3,2,1,0:T(8,128)(2,1)}, u32[]{:S(2)}, u32[]{:S(2)}) async-start(bf16[4,2,64,1536]{3,2,1,0:T(8,128)(2,1)} %copy.67), calls=%async_computation.2 | async-start | bytes 3145728 | tf_op jit(solution)/shard_map/all_to_all | solution.py:165
Sparse Core Ops, SparseCore 0:
  9.6 39.7 all-gather.2
  54.6 27.0 all-gather.4
  88.5 35.2 reduce-scatter.1
